TPU v7x, 32 devices: a whole 2x2x4 slice. The times are simulated.
32 devices in a mesh: groups: 2 (over y), tile: 16 (over z, x, core).
Axes of the slice: x: 2, y: 2, z: 4, core: 2. Of those that a mesh axis runs over, the one named last changes fastest.
Arguments:
- log_demand: float32 [512, 256], P(('groups', 'tile')), parts along dimension 0, may hold values from -3 to 0
- log_capacity: float32 [32, 256], P(('groups', 'tile')), parts along dimension 0, may hold values from -1 to 1
- warm_potential: float32 [32, 256], P(('groups', 'tile')), parts along dimension 0, may hold values from -4 to 4
- facility_xy: float32 [32, 2, 256], P('groups'), parts along dimension 0, may hold values from 0 to 1472
- pair_block: int32 [512, 16], P(('groups', 'tile')), parts along dimension 0, may hold values from 0 to 15, as said below
- pair_count: int32 [512], P(('groups', 'tile')), parts along dimension 0, may hold values from 1 to 16, as said below
Outputs:
- cell_potential: float32 [512, 256], P(('groups', 'tile')), parts along dimension 0
- facility_potential: float32 [32, 256], P(('groups', 'tile')), parts along dimension 0
There are 2 independent parts, one for each index of `groups`. A program takes and returns all parts, laid end to end along the dimension named above; each array names one. Nothing has to cross between parts.
Inputs may be any that keep to these rules, and one draw needn't show every extreme that they name: `pair_count`: every tile has at least one active pair and some tile has 16. `pair_block`: the 16 slots of a tile name distinct blocks; slot 0 is the block of the tile's own tile row (block b belongs to tile row b); every slot's block b satisfies |b - floor(t / 16)| <= 16 for its tile t; slots at or beyond the tile's pair_count are ignored.
All inputs are finite; a program needn't handle non-finite values.
Results may differ from a plain program's by a relative error of at most 0.0003.
Values sent between devices are 32-bit elements; how exact they have to be, the bound alone decides.
A program may use at most 64 MiB of HBM per device.

v0:
```python
import jax
import jax.numpy as jnp
from jax import lax
from jax.sharding import PartitionSpec as P

TSIDE = 16
TILE_COLS = 16
KSLOTS = 16
ITERS = 2
REACH = 64
SPAN = 16


LOWEST = -1e30


def from_behind(block, axis, distance):
    devices = range(lax.axis_size(axis))
    route = [(i - distance, i) for i in devices if i - distance in devices]
    return lax.ppermute(block, axis, route)


def cell_coords(tile_index):
    cell_ids = jnp.arange(TSIDE * TSIDE, dtype=jnp.int32)
    column = tile_index % TILE_COLS * TSIDE + cell_ids % TSIDE
    row_cell = tile_index // TILE_COLS * TSIDE + cell_ids // TSIDE
    return (column.astype(jnp.float32) + 0.5, row_cell.astype(jnp.float32) + 0.5)


def pair_cost(coord_x, coord_y, positions):
    delta_x = coord_x[None, :, None] - positions[:, 0, :][:, None, :]
    delta_y = coord_y[None, :, None] - positions[:, 1, :][:, None, :]
    return (delta_x * delta_x + delta_y * delta_y) / float(REACH * REACH)


def tile_pass(tile_index, demand_row, potentials, positions, active):
    coord_x, coord_y = cell_coords(tile_index)
    pair_costs = pair_cost(coord_x, coord_y, positions)
    scores = jnp.where(active[:, None, None], potentials[:, None, :] - pair_costs, LOWEST)
    row_top = jnp.max(scores, axis=(0, 2))
    row_sum = jnp.sum(jnp.exp(scores - row_top[None, :, None]), axis=(0, 2))
    cell_pot = demand_row - (row_top + jnp.log(row_sum))
    column_scores = cell_pot[None, :, None] - pair_costs
    col_top = jnp.max(column_scores, axis=1)
    col_sum = jnp.sum(jnp.exp(column_scores - col_top[:, None, :]), axis=1)
    col_top = jnp.where(active[:, None], col_top, LOWEST)
    col_sum = jnp.where(active[:, None], col_sum, 0.0)
    return (cell_pot, col_top, col_sum)


def merge_parts(top_a, sum_a, top_b, sum_b):
    top_new = jnp.maximum(top_a, top_b)
    return (top_new, sum_a * jnp.exp(top_a - top_new) + sum_b * jnp.exp(top_b - top_new))


def on_device(log_demand, log_capacity, warm_potential, facility_xy, pair_block, pair_count):
    tiles_here = log_demand.shape[0]
    blocks_here = log_capacity.shape[0]
    block_width = log_capacity.shape[1]
    devices_along = lax.axis_size("tile")
    my_index = lax.axis_index("tile")
    reach = min(devices_along - 1, (SPAN + blocks_here - 1) // blocks_here)
    window = 2 * reach + 1
    tile_ids = my_index * tiles_here + jnp.arange(tiles_here, dtype=jnp.int32)
    slot_ids = jnp.arange(KSLOTS, dtype=jnp.int32)
    first_block = (my_index - reach) * blocks_here
    local_block = pair_block - first_block
    facility_pot = warm_potential
    cell_pot = log_demand
    for step_index in range(ITERS):
        slabs = []
        for position in range(window):
            distance = reach - position
            if distance == 0:
                slabs.append(facility_pot)
            else:
                slabs.append(from_behind(facility_pot, "tile", distance))
        window_pot = jnp.concatenate(slabs, axis=0)

        def one_tile(inputs):
            tile_index, demand_row, blocks, nearby, slot_limit = inputs
            active = slot_ids < slot_limit
            return tile_pass(
                tile_index, demand_row, window_pot[nearby], facility_xy[blocks], active
            )

        cell_pot, col_top, col_sum = lax.map(
            one_tile, (tile_ids, log_demand, pair_block, local_block, pair_count)
        )
        flat_ids = local_block.reshape(-1)
        flat_top = col_top.reshape(-1, block_width)
        flat_sum = col_sum.reshape(-1, block_width)
        local_top = (
            jnp.full((window * blocks_here, block_width), LOWEST, jnp.float32)
            .at[flat_ids]
            .max(flat_top)
        )
        local_sum = (
            jnp.zeros((window * blocks_here, block_width), jnp.float32)
            .at[flat_ids]
            .add(flat_sum * jnp.exp(flat_top - local_top[flat_ids]))
        )

        def slab_of(position):
            return (
                local_top[position * blocks_here : (position + 1) * blocks_here],
                local_sum[position * blocks_here : (position + 1) * blocks_here],
            )

        own_top, block_sum = slab_of(reach)
        for distance in range(-reach, reach + 1):
            if distance != 0:
                send_top, send_sum = slab_of(reach + distance)
                got_top, got_sum = from_behind((send_top, send_sum), "tile", distance)
                source = my_index - distance
                valid = (source >= 0) & (source < devices_along)
                got_top = jnp.where(valid, got_top, LOWEST)
                got_sum = jnp.where(valid, got_sum, 0.0)
                own_top, block_sum = merge_parts(own_top, block_sum, got_top, got_sum)
        facility_pot = log_capacity - (own_top + jnp.log(block_sum))
    return (cell_pot, facility_pot)


def solution(mesh):
    placed = (
        P(("groups", "tile"), None),
        P(("groups", "tile"), None),
        P(("groups", "tile"), None),
        P("groups", None, None),
        P(("groups", "tile"), None),
        P(("groups", "tile")),
    )
    return jax.shard_map(
        on_device,
        mesh=mesh,
        in_specs=placed,
        out_specs=(P(("groups", "tile"), None), P(("groups", "tile"), None)),
        check_vma=False,
    )
```

profile of v0, /device:TPU:0, one launch (start us, length us, event | category | flops | bytes accessed | tf_op | source)
XLA Modules:
  0.0 832.8 jit_solution(4137859479045331866)
XLA Ops:
  0.6 7.3 collective-permute-start
  11.9 2.4 collective-permute-start.12
  15.1 4.0 collective-permute-start.13
  27.2 11.6 %collective-permute-start.2 = (f32[1,256]{1,0:T(1,128)}, f32[1,256]{1,0:T(1,128)S(1)}, u32[]{:S(2)}, u32[]{:S(2)}) collective-permute-start(f32[1,256]{1,0:T(1,128)} %param.12), channel_id=1, source_target_pairs={{0,13},{1,14},{2,15},{16,29},{17,30},{18,31}} | collective-permute-start | bytes 3080 | tf_op jit(solution)/shard_map/ppermute | solution.py:20
  54.3 3.6 collective-permute-start.3
  63.2 6.2 collective-permute-start.8
  74.0 214.7 %while.34 = (s32[]{:T(128)}, f32[16,16,256]{2,1,0:T(8,128)S(1)}, f32[16,16,256]{2,1,0:T(8,128)S(1)}, s32[16]{0:T(128)S(1)}, f32[16,256]{1,0:T(8,128)}, /*index=5...) while((s32[]{:T(128)}, f32[16,16,256]{2,1,0:T(8,128)S(1)}, ...), condition=%wide.region_5.6_spmd.clone, body=%wide.region_0.5_spmd.clone.sunk | while | flops 37755528 | bytes 539080 | solution.py:87
  288.7 2.1 scatter_custom_fusion
  291.9 2.0 scatter_custom_fusion.1
  299.1 3.0 collective-permute-start.75
  302.2 4.8 collective-permute-start.76
  307.0 5.6 collective-permute-start.77
  312.6 3.3 collective-permute-start.78
  315.9 3.1 collective-permute-start.79
  319.0 3.1 collective-permute-start.80
  323.5 2.2 collective-permute-start.82
  356.2 3.0 collective-permute-start.45
  360.6 3.7 collective-permute-start.46
  364.3 5.4 collective-permute-start.47
  369.7 5.3 collective-permute-start.48
  374.9 3.1 collective-permute-start.49
  378.1 3.1 collective-permute-start.50
  382.6 2.2 collective-permute-start.52
  414.4 4.1 collective-permute-start.100
  418.5 3.9 collective-permute-start.101
  422.4 3.8 collective-permute-start.102
  426.2 2.6 collective-permute-start.103
  441.6 2.7 collective-permute-done.108
  456.7 8.0 collective-permute-start.90
  474.0 3.2 collective-permute-start.98
  477.2 2.4 collective-permute-start.99
  480.8 226.6 %while.35 = (s32[]{:T(128)}, f32[16,256]{1,0:T(8,128)S(1)}, f32[16,16,256]{2,1,0:T(8,128)S(1)}, f32[16,16,256]{2,1,0:T(8,128)S(1)}, f32[16,256]{1,0:T(8,128)}, /...) while((s32[]{:T(128)}, f32[16,256]{1,0:T(8,128)S(1)}, ...), condition=%wide.region_13.14_spmd.clone, body=%wide.region_8.13_spmd.clone.sunk | while | flops 37755784 | bytes 545240 | solution.py:87
  707.4 2.0 scatter_custom_fusion.2
  710.4 2.0 scatter_custom_fusion.3
  717.6 3.0 collective-permute-start.165
  720.7 4.8 collective-permute-start.166
  725.5 5.6 collective-permute-start.167
  731.1 3.3 collective-permute-start.168
  734.4 2.8 collective-permute-start.169
  737.2 3.1 collective-permute-start.170
  741.7 2.0 collective-permute-start.172
  774.1 3.0 collective-permute-start.135
  778.5 3.7 collective-permute-start.136
  782.2 5.4 collective-permute-start.137
  787.6 5.3 collective-permute-start.138
  792.9 3.1 collective-permute-start.139
  796.0 3.1 collective-permute-start.140
  800.5 2.2 collective-permute-start.142
  (992 shorter events, 568.0 us)
Async XLA Ops:
  0.6 14.4 %collective-permute-start = (f32[1,256]{1,0:T(1,128)}, f32[1,256]{1,0:T(1,128)S(1)}, u32[]{:S(2)}, u32[]{:S(2)}) collective-permute-start(f32[1,256]{1,0:T(1,128)} %param.12), channel_id=1, source_target_pairs={{0,15},{16,31}} | collective-permute-start | bytes 3080 | tf_op jit(solution)/shard_map/ppermute | solution.py:20
  9.3 11.3 %collective-permute-start.10 = (f32[1,256]{1,0:T(1,128)}, f32[1,256]{1,0:T(1,128)S(1)}, u32[]{:S(2)}, u32[]{:S(2)}) collective-permute-start(f32[1,256]{1,0:T(1,128)} %param.12), channel_id=1, source_target_pairs={{0,5},{1,6},{2,7},{3,8},{4,9},{5,10},{6,11},{7,12},{8,13},{9,14},{... | collective-permute-start | bytes 3080 | tf_op jit(solution)/shard_map/ppermute | solution.py:20
  10.6 11.4 %collective-permute-start.11 = (f32[1,256]{1,0:T(1,128)}, f32[1,256]{1,0:T(1,128)S(1)}, u32[]{:S(2)}, u32[]{:S(2)}) collective-permute-start(f32[1,256]{1,0:T(1,128)} %param.12), channel_id=1, source_target_pairs={{0,4},{1,5},{2,6},{3,7},{4,8},{5,9},{6,10},{7,11},{8,12},{9,13},{1... | collective-permute-start | bytes 3080 | tf_op jit(solution)/shard_map/ppermute | solution.py:20
  11.9 11.4 %collective-permute-start.12 = (f32[1,256]{1,0:T(1,128)}, f32[1,256]{1,0:T(1,128)S(1)}, u32[]{:S(2)}, u32[]{:S(2)}) collective-permute-start(f32[1,256]{1,0:T(1,128)} %param.12), channel_id=1, source_target_pairs={{0,3},{1,4},{2,5},{3,6},{4,7},{5,8},{6,9},{7,10},{8,11},{9,12},{10... | collective-permute-start | bytes 3080 | tf_op jit(solution)/shard_map/ppermute | solution.py:20
  21.9 16.8 %collective-permute-start.16 = (f32[1,256]{1,0:T(1,128)}, f32[1,256]{1,0:T(1,128)S(1)}, u32[]{:S(2)}, u32[]{:S(2)}) collective-permute-start(f32[1,256]{1,0:T(1,128)} %param.12), channel_id=1, source_target_pairs={{2,0},{3,1},{4,2},{5,3},{6,4},{7,5},{8,6},{9,7},{10,8},{11,9},{12,... | collective-permute-start | bytes 3080 | tf_op jit(solution)/shard_map/ppermute | solution.py:20
  23.2 16.8 %collective-permute-start.17 = (f32[1,256]{1,0:T(1,128)}, f32[1,256]{1,0:T(1,128)S(1)}, u32[]{:S(2)}, u32[]{:S(2)}) collective-permute-start(f32[1,256]{1,0:T(1,128)} %param.12), channel_id=1, source_target_pairs={{3,0},{4,1},{5,2},{6,3},{7,4},{8,5},{9,6},{10,7},{11,8},{12,9},{13... | collective-permute-start | bytes 3080 | tf_op jit(solution)/shard_map/ppermute | solution.py:20
  24.6 16.8 %collective-permute-start.18 = (f32[1,256]{1,0:T(1,128)}, f32[1,256]{1,0:T(1,128)S(1)}, u32[]{:S(2)}, u32[]{:S(2)}) collective-permute-start(f32[1,256]{1,0:T(1,128)} %param.12), channel_id=1, source_target_pairs={{4,0},{5,1},{6,2},{7,3},{8,4},{9,5},{10,6},{11,7},{12,8},{13,9},{1... | collective-permute-start | bytes 3080 | tf_op jit(solution)/shard_map/ppermute | solution.py:20
  25.9 16.8 %collective-permute-start.19 = (f32[1,256]{1,0:T(1,128)}, f32[1,256]{1,0:T(1,128)S(1)}, u32[]{:S(2)}, u32[]{:S(2)}) collective-permute-start(f32[1,256]{1,0:T(1,128)} %param.12), channel_id=1, source_target_pairs={{5,0},{6,1},{7,2},{8,3},{9,4},{10,5},{11,6},{12,7},{13,8},{14,9},{... | collective-permute-start | bytes 3080 | tf_op jit(solution)/shard_map/ppermute | solution.py:20
  27.2 16.8 %collective-permute-start.2 = (f32[1,256]{1,0:T(1,128)}, f32[1,256]{1,0:T(1,128)S(1)}, u32[]{:S(2)}, u32[]{:S(2)}) collective-permute-start(f32[1,256]{1,0:T(1,128)} %param.12), channel_id=1, source_target_pairs={{0,13},{1,14},{2,15},{16,29},{17,30},{18,31}} | collective-permute-start | bytes 3080 | tf_op jit(solution)/shard_map/ppermute | solution.py:20
  58.0 11.4 %collective-permute-start.4 = (f32[1,256]{1,0:T(1,128)}, f32[1,256]{1,0:T(1,128)S(1)}, u32[]{:S(2)}, u32[]{:S(2)}) collective-permute-start(f32[1,256]{1,0:T(1,128)} %param.12), channel_id=1, source_target_pairs={{0,11},{1,12},{2,13},{3,14},{4,15},{16,27},{17,28},{18,29},{19,30}... | collective-permute-start | bytes 3080 | tf_op jit(solution)/shard_map/ppermute | solution.py:20
  59.3 11.7 %collective-permute-start.5 = (f32[1,256]{1,0:T(1,128)}, f32[1,256]{1,0:T(1,128)S(1)}, u32[]{:S(2)}, u32[]{:S(2)}) collective-permute-start(f32[1,256]{1,0:T(1,128)} %param.12), channel_id=1, source_target_pairs={{0,10},{1,11},{2,12},{3,13},{4,14},{5,15},{16,26},{17,27},{18,28},... | collective-permute-start | bytes 3080 | tf_op jit(solution)/shard_map/ppermute | solution.py:20
  295.2 11.8 %collective-permute-start.72 = (f32[1,256]{1,0:T(1,128)S(1)}, f32[1,256]{1,0:T(1,128)S(1)}, u32[]{:S(2)}, u32[]{:S(2)}) collective-permute-start(f32[1,256]{1,0:T(1,128)S(1)} %get-tuple-element.586), channel_id=1, source_target_pairs={{3,0},{4,1},{5,2},{6,3},{7,4},{8,5},{9,6},{10,7},{11,8},{12,9},{13... | collective-permute-start | bytes 3080 | tf_op jit(solution)/shard_map/ppermute | solution.py:20
  296.5 16.1 %collective-permute-start.73 = (f32[1,256]{1,0:T(1,128)S(1)}, f32[1,256]{1,0:T(1,128)S(1)}, u32[]{:S(2)}, u32[]{:S(2)}) collective-permute-start(f32[1,256]{1,0:T(1,128)S(1)} %get-tuple-element.585), channel_id=1, source_target_pairs={{2,0},{3,1},{4,2},{5,3},{6,4},{7,5},{8,6},{9,7},{10,8},{11,9},{12,... | collective-permute-start | bytes 3080 | tf_op jit(solution)/shard_map/ppermute | solution.py:20
  297.8 18.1 %collective-permute-start.74 = (f32[1,256]{1,0:T(1,128)S(1)}, f32[1,256]{1,0:T(1,128)S(1)}, u32[]{:S(2)}, u32[]{:S(2)}) collective-permute-start(f32[1,256]{1,0:T(1,128)S(1)} %get-tuple-element.584), channel_id=1, source_target_pairs={{1,0},{2,1},{3,2},{4,3},{5,4},{6,5},{7,6},{8,7},{9,8},{10,9},{11,1... | collective-permute-start | bytes 3080 | tf_op jit(solution)/shard_map/ppermute | solution.py:20
  299.1 19.9 %collective-permute-start.75 = (f32[1,256]{1,0:T(1,128)S(1)}, f32[1,256]{1,0:T(1,128)S(1)}, u32[]{:S(2)}, u32[]{:S(2)}) collective-permute-start(f32[1,256]{1,0:T(1,128)S(1)} %get-tuple-element.583), channel_id=1, source_target_pairs={{0,1},{1,2},{2,3},{3,4},{4,5},{5,6},{6,7},{7,8},{8,9},{9,10},{10,1... | collective-permute-start | bytes 3080 | tf_op jit(solution)/shard_map/ppermute | solution.py:20
  302.2 20.0 %collective-permute-start.76 = (f32[1,256]{1,0:T(1,128)S(1)}, f32[1,256]{1,0:T(1,128)S(1)}, u32[]{:S(2)}, u32[]{:S(2)}) collective-permute-start(f32[1,256]{1,0:T(1,128)S(1)} %get-tuple-element.582), channel_id=1, source_target_pairs={{0,2},{1,3},{2,4},{3,5},{4,6},{5,7},{6,8},{7,9},{8,10},{9,11},{10,... | collective-permute-start | bytes 3080 | tf_op jit(solution)/shard_map/ppermute | solution.py:20
  307.0 16.5 %collective-permute-start.77 = (f32[1,256]{1,0:T(1,128)S(1)}, f32[1,256]{1,0:T(1,128)S(1)}, u32[]{:S(2)}, u32[]{:S(2)}) collective-permute-start(f32[1,256]{1,0:T(1,128)S(1)} %get-tuple-element.581), channel_id=1, source_target_pairs={{0,3},{1,4},{2,5},{3,6},{4,7},{5,8},{6,9},{7,10},{8,11},{9,12},{10... | collective-permute-start | bytes 3080 | tf_op jit(solution)/shard_map/ppermute | solution.py:20
  312.6 13.1 %collective-permute-start.78 = (f32[1,256]{1,0:T(1,128)S(1)}, f32[1,256]{1,0:T(1,128)S(1)}, u32[]{:S(2)}, u32[]{:S(2)}) collective-permute-start(f32[1,256]{1,0:T(1,128)S(1)} %get-tuple-element.580), channel_id=1, source_target_pairs={{0,4},{1,5},{2,6},{3,7},{4,8},{5,9},{6,10},{7,11},{8,12},{9,13},{1... | collective-permute-start | bytes 3080 | tf_op jit(solution)/shard_map/ppermute | solution.py:20
  352.3 12.0 %collective-permute-start.42 = (f32[1,256]{1,0:T(1,128)S(1)}, f32[1,256]{1,0:T(1,128)S(1)}, u32[]{:S(2)}, u32[]{:S(2)}) collective-permute-start(f32[1,256]{1,0:T(1,128)S(1)} %get-tuple-element.556), channel_id=1, source_target_pairs={{3,0},{4,1},{5,2},{6,3},{7,4},{8,5},{9,6},{10,7},{11,8},{12,9},{13... | collective-permute-start | bytes 3080 | tf_op jit(solution)/shard_map/ppermute | solution.py:20
  353.6 16.1 %collective-permute-start.43 = (f32[1,256]{1,0:T(1,128)S(1)}, f32[1,256]{1,0:T(1,128)S(1)}, u32[]{:S(2)}, u32[]{:S(2)}) collective-permute-start(f32[1,256]{1,0:T(1,128)S(1)} %get-tuple-element.555), channel_id=1, source_target_pairs={{2,0},{3,1},{4,2},{5,3},{6,4},{7,5},{8,6},{9,7},{10,8},{11,9},{12,... | collective-permute-start | bytes 3080 | tf_op jit(solution)/shard_map/ppermute | solution.py:20
  354.9 20.1 %collective-permute-start.44 = (f32[1,256]{1,0:T(1,128)S(1)}, f32[1,256]{1,0:T(1,128)S(1)}, u32[]{:S(2)}, u32[]{:S(2)}) collective-permute-start(f32[1,256]{1,0:T(1,128)S(1)} %get-tuple-element.554), channel_id=1, source_target_pairs={{1,0},{2,1},{3,2},{4,3},{5,4},{6,5},{7,6},{8,7},{9,8},{10,9},{11,1... | collective-permute-start | bytes 3080 | tf_op jit(solution)/shard_map/ppermute | solution.py:20
  356.2 21.9 %collective-permute-start.45 = (f32[1,256]{1,0:T(1,128)S(1)}, f32[1,256]{1,0:T(1,128)S(1)}, u32[]{:S(2)}, u32[]{:S(2)}) collective-permute-start(f32[1,256]{1,0:T(1,128)S(1)} %get-tuple-element.553), channel_id=1, source_target_pairs={{0,1},{1,2},{2,3},{3,4},{4,5},{5,6},{6,7},{7,8},{8,9},{9,10},{10,1... | collective-permute-start | bytes 3080 | tf_op jit(solution)/shard_map/ppermute | solution.py:20
  360.6 20.6 %collective-permute-start.46 = (f32[1,256]{1,0:T(1,128)S(1)}, f32[1,256]{1,0:T(1,128)S(1)}, u32[]{:S(2)}, u32[]{:S(2)}) collective-permute-start(f32[1,256]{1,0:T(1,128)S(1)} %get-tuple-element.552), channel_id=1, source_target_pairs={{0,2},{1,3},{2,4},{3,5},{4,6},{5,7},{6,8},{7,9},{8,10},{9,11},{10,... | collective-permute-start | bytes 3080 | tf_op jit(solution)/shard_map/ppermute | solution.py:20
  364.3 18.3 %collective-permute-start.47 = (f32[1,256]{1,0:T(1,128)S(1)}, f32[1,256]{1,0:T(1,128)S(1)}, u32[]{:S(2)}, u32[]{:S(2)}) collective-permute-start(f32[1,256]{1,0:T(1,128)S(1)} %get-tuple-element.551), channel_id=1, source_target_pairs={{0,3},{1,4},{2,5},{3,6},{4,7},{5,8},{6,9},{7,10},{8,11},{9,12},{10... | collective-permute-start | bytes 3080 | tf_op jit(solution)/shard_map/ppermute | solution.py:20
  369.7 15.1 %collective-permute-start.48 = (f32[1,256]{1,0:T(1,128)S(1)}, f32[1,256]{1,0:T(1,128)S(1)}, u32[]{:S(2)}, u32[]{:S(2)}) collective-permute-start(f32[1,256]{1,0:T(1,128)S(1)} %get-tuple-element.550), channel_id=1, source_target_pairs={{0,4},{1,5},{2,6},{3,7},{4,8},{5,9},{6,10},{7,11},{8,12},{9,13},{1... | collective-permute-start | bytes 3080 | tf_op jit(solution)/shard_map/ppermute | solution.py:20
  414.4 15.8 %collective-permute-start.100 = (f32[1,256]{1,0:T(1,128)S(1)}, f32[1,256]{1,0:T(1,128)S(1)}, u32[]{:S(2)}, u32[]{:S(2)}) collective-permute-start(f32[1,256]{1,0:T(1,128)S(1)} %add_subtract_fusion.2), channel_id=1, source_target_pairs={{0,5},{1,6},{2,7},{3,8},{4,9},{5,10},{6,11},{7,12},{8,13},{9,14},{... | collective-permute-start | bytes 3080 | tf_op jit(solution)/shard_map/ppermute | solution.py:20
  418.5 13.0 %collective-permute-start.101 = (f32[1,256]{1,0:T(1,128)S(1)}, f32[1,256]{1,0:T(1,128)S(1)}, u32[]{:S(2)}, u32[]{:S(2)}) collective-permute-start(f32[1,256]{1,0:T(1,128)S(1)} %add_subtract_fusion.2), channel_id=1, source_target_pairs={{0,4},{1,5},{2,6},{3,7},{4,8},{5,9},{6,10},{7,11},{8,12},{9,13},{1... | collective-permute-start | bytes 3080 | tf_op jit(solution)/shard_map/ppermute | solution.py:20
  438.9 12.0 %collective-permute-start.111 = (f32[1,256]{1,0:T(1,128)S(1)}, f32[1,256]{1,0:T(1,128)S(1)}, u32[]{:S(2)}, u32[]{:S(2)}) collective-permute-start(f32[1,256]{1,0:T(1,128)S(1)} %add_subtract_fusion.2), channel_id=1, source_target_pairs={{7,0},{8,1},{9,2},{10,3},{11,4},{12,5},{13,6},{14,7},{15,8},{23,16... | collective-permute-start | bytes 3080 | tf_op jit(solution)/shard_map/ppermute | solution.py:20
  440.3 12.5 %collective-permute-start.112 = (f32[1,256]{1,0:T(1,128)S(1)}, f32[1,256]{1,0:T(1,128)S(1)}, u32[]{:S(2)}, u32[]{:S(2)}) collective-permute-start(f32[1,256]{1,0:T(1,128)S(1)} %add_subtract_fusion.2), channel_id=1, source_target_pairs={{8,0},{9,1},{10,2},{11,3},{12,4},{13,5},{14,6},{15,7},{24,16},{25,... | collective-permute-start | bytes 3080 | tf_op jit(solution)/shard_map/ppermute | solution.py:20
  450.9 13.9 %collective-permute-start.116 = (f32[1,256]{1,0:T(1,128)S(1)}, f32[1,256]{1,0:T(1,128)S(1)}, u32[]{:S(2)}, u32[]{:S(2)}) collective-permute-start(f32[1,256]{1,0:T(1,128)S(1)} %add_subtract_fusion.2), channel_id=1, source_target_pairs={{12,0},{13,1},{14,2},{15,3},{28,16},{29,17},{30,18},{31,19}} | collective-permute-start | bytes 3080 | tf_op jit(solution)/shard_map/ppermute | solution.py:20
  452.8 13.3 %collective-permute-start.117 = (f32[1,256]{1,0:T(1,128)S(1)}, f32[1,256]{1,0:T(1,128)S(1)}, u32[]{:S(2)}, u32[]{:S(2)}) collective-permute-start(f32[1,256]{1,0:T(1,128)S(1)} %add_subtract_fusion.2), channel_id=1, source_target_pairs={{13,0},{14,1},{15,2},{29,16},{30,17},{31,18}} | collective-permute-start | bytes 3080 | tf_op jit(solution)/shard_map/ppermute | solution.py:20
  454.1 13.3 %collective-permute-start.118 = (f32[1,256]{1,0:T(1,128)S(1)}, f32[1,256]{1,0:T(1,128)S(1)}, u32[]{:S(2)}, u32[]{:S(2)}) collective-permute-start(f32[1,256]{1,0:T(1,128)S(1)} %add_subtract_fusion.2), channel_id=1, source_target_pairs={{14,0},{15,1},{30,16},{31,17}} | collective-permute-start | bytes 3080 | tf_op jit(solution)/shard_map/ppermute | solution.py:20
  455.4 13.3 %collective-permute-start.119 = (f32[1,256]{1,0:T(1,128)S(1)}, f32[1,256]{1,0:T(1,128)S(1)}, u32[]{:S(2)}, u32[]{:S(2)}) collective-permute-start(f32[1,256]{1,0:T(1,128)S(1)} %add_subtract_fusion.2), channel_id=1, source_target_pairs={{15,0},{31,16}} | collective-permute-start | bytes 3080 | tf_op jit(solution)/shard_map/ppermute | solution.py:20
  456.7 13.3 %collective-permute-start.90 = (f32[1,256]{1,0:T(1,128)S(1)}, f32[1,256]{1,0:T(1,128)S(1)}, u32[]{:S(2)}, u32[]{:S(2)}) collective-permute-start(f32[1,256]{1,0:T(1,128)S(1)} %add_subtract_fusion.2), channel_id=1, source_target_pairs={{0,15},{16,31}} | collective-permute-start | bytes 3080 | tf_op jit(solution)/shard_map/ppermute | solution.py:20
  713.7 11.8 %collective-permute-start.162 = (f32[1,256]{1,0:T(1,128)S(1)}, f32[1,256]{1,0:T(1,128)S(1)}, u32[]{:S(2)}, u32[]{:S(2)}) collective-permute-start(f32[1,256]{1,0:T(1,128)S(1)} %get-tuple-element.526), channel_id=1, source_target_pairs={{3,0},{4,1},{5,2},{6,3},{7,4},{8,5},{9,6},{10,7},{11,8},{12,9},{13... | collective-permute-start | bytes 3080 | tf_op jit(solution)/shard_map/ppermute | solution.py:20
  715.0 16.1 %collective-permute-start.163 = (f32[1,256]{1,0:T(1,128)S(1)}, f32[1,256]{1,0:T(1,128)S(1)}, u32[]{:S(2)}, u32[]{:S(2)}) collective-permute-start(f32[1,256]{1,0:T(1,128)S(1)} %get-tuple-element.525), channel_id=1, source_target_pairs={{2,0},{3,1},{4,2},{5,3},{6,4},{7,5},{8,6},{9,7},{10,8},{11,9},{12,... | collective-permute-start | bytes 3080 | tf_op jit(solution)/shard_map/ppermute | solution.py:20
  716.3 18.1 %collective-permute-start.164 = (f32[1,256]{1,0:T(1,128)S(1)}, f32[1,256]{1,0:T(1,128)S(1)}, u32[]{:S(2)}, u32[]{:S(2)}) collective-permute-start(f32[1,256]{1,0:T(1,128)S(1)} %get-tuple-element.524), channel_id=1, source_target_pairs={{1,0},{2,1},{3,2},{4,3},{5,4},{6,5},{7,6},{8,7},{9,8},{10,9},{11,1... | collective-permute-start | bytes 3080 | tf_op jit(solution)/shard_map/ppermute | solution.py:20
  717.6 19.6 %collective-permute-start.165 = (f32[1,256]{1,0:T(1,128)S(1)}, f32[1,256]{1,0:T(1,128)S(1)}, u32[]{:S(2)}, u32[]{:S(2)}) collective-permute-start(f32[1,256]{1,0:T(1,128)S(1)} %get-tuple-element.523), channel_id=1, source_target_pairs={{0,1},{1,2},{2,3},{3,4},{4,5},{5,6},{6,7},{7,8},{8,9},{9,10},{10,1... | collective-permute-start | bytes 3080 | tf_op jit(solution)/shard_map/ppermute | solution.py:20
  720.7 19.7 %collective-permute-start.166 = (f32[1,256]{1,0:T(1,128)S(1)}, f32[1,256]{1,0:T(1,128)S(1)}, u32[]{:S(2)}, u32[]{:S(2)}) collective-permute-start(f32[1,256]{1,0:T(1,128)S(1)} %get-tuple-element.522), channel_id=1, source_target_pairs={{0,2},{1,3},{2,4},{3,5},{4,6},{5,7},{6,8},{7,9},{8,10},{9,11},{10,... | collective-permute-start | bytes 3080 | tf_op jit(solution)/shard_map/ppermute | solution.py:20
  725.5 16.2 %collective-permute-start.167 = (f32[1,256]{1,0:T(1,128)S(1)}, f32[1,256]{1,0:T(1,128)S(1)}, u32[]{:S(2)}, u32[]{:S(2)}) collective-permute-start(f32[1,256]{1,0:T(1,128)S(1)} %get-tuple-element.521), channel_id=1, source_target_pairs={{0,3},{1,4},{2,5},{3,6},{4,7},{5,8},{6,9},{7,10},{8,11},{9,12},{10... | collective-permute-start | bytes 3080 | tf_op jit(solution)/shard_map/ppermute | solution.py:20
  731.1 12.5 %collective-permute-start.168 = (f32[1,256]{1,0:T(1,128)S(1)}, f32[1,256]{1,0:T(1,128)S(1)}, u32[]{:S(2)}, u32[]{:S(2)}) collective-permute-start(f32[1,256]{1,0:T(1,128)S(1)} %get-tuple-element.520), channel_id=1, source_target_pairs={{0,4},{1,5},{2,6},{3,7},{4,8},{5,9},{6,10},{7,11},{8,12},{9,13},{1... | collective-permute-start | bytes 3080 | tf_op jit(solution)/shard_map/ppermute | solution.py:20
  770.2 12.0 %collective-permute-start.132 = (f32[1,256]{1,0:T(1,128)S(1)}, f32[1,256]{1,0:T(1,128)S(1)}, u32[]{:S(2)}, u32[]{:S(2)}) collective-permute-start(f32[1,256]{1,0:T(1,128)S(1)} %get-tuple-element.496), channel_id=1, source_target_pairs={{3,0},{4,1},{5,2},{6,3},{7,4},{8,5},{9,6},{10,7},{11,8},{12,9},{13... | collective-permute-start | bytes 3080 | tf_op jit(solution)/shard_map/ppermute | solution.py:20
  771.5 16.1 %collective-permute-start.133 = (f32[1,256]{1,0:T(1,128)S(1)}, f32[1,256]{1,0:T(1,128)S(1)}, u32[]{:S(2)}, u32[]{:S(2)}) collective-permute-start(f32[1,256]{1,0:T(1,128)S(1)} %get-tuple-element.495), channel_id=1, source_target_pairs={{2,0},{3,1},{4,2},{5,3},{6,4},{7,5},{8,6},{9,7},{10,8},{11,9},{12,... | collective-permute-start | bytes 3080 | tf_op jit(solution)/shard_map/ppermute | solution.py:20
  772.8 20.1 %collective-permute-start.134 = (f32[1,256]{1,0:T(1,128)S(1)}, f32[1,256]{1,0:T(1,128)S(1)}, u32[]{:S(2)}, u32[]{:S(2)}) collective-permute-start(f32[1,256]{1,0:T(1,128)S(1)} %get-tuple-element.494), channel_id=1, source_target_pairs={{1,0},{2,1},{3,2},{4,3},{5,4},{6,5},{7,6},{8,7},{9,8},{10,9},{11,1... | collective-permute-start | bytes 3080 | tf_op jit(solution)/shard_map/ppermute | solution.py:20
  774.1 21.9 %collective-permute-start.135 = (f32[1,256]{1,0:T(1,128)S(1)}, f32[1,256]{1,0:T(1,128)S(1)}, u32[]{:S(2)}, u32[]{:S(2)}) collective-permute-start(f32[1,256]{1,0:T(1,128)S(1)} %get-tuple-element.493), channel_id=1, source_target_pairs={{0,1},{1,2},{2,3},{3,4},{4,5},{5,6},{6,7},{7,8},{8,9},{9,10},{10,1... | collective-permute-start | bytes 3080 | tf_op jit(solution)/shard_map/ppermute | solution.py:20
  778.5 20.6 %collective-permute-start.136 = (f32[1,256]{1,0:T(1,128)S(1)}, f32[1,256]{1,0:T(1,128)S(1)}, u32[]{:S(2)}, u32[]{:S(2)}) collective-permute-start(f32[1,256]{1,0:T(1,128)S(1)} %get-tuple-element.492), channel_id=1, source_target_pairs={{0,2},{1,3},{2,4},{3,5},{4,6},{5,7},{6,8},{7,9},{8,10},{9,11},{10,... | collective-permute-start | bytes 3080 | tf_op jit(solution)/shard_map/ppermute | solution.py:20
  782.2 18.3 %collective-permute-start.137 = (f32[1,256]{1,0:T(1,128)S(1)}, f32[1,256]{1,0:T(1,128)S(1)}, u32[]{:S(2)}, u32[]{:S(2)}) collective-permute-start(f32[1,256]{1,0:T(1,128)S(1)} %get-tuple-element.491), channel_id=1, source_target_pairs={{0,3},{1,4},{2,5},{3,6},{4,7},{5,8},{6,9},{7,10},{8,11},{9,12},{10... | collective-permute-start | bytes 3080 | tf_op jit(solution)/shard_map/ppermute | solution.py:20
  787.6 15.1 %collective-permute-start.138 = (f32[1,256]{1,0:T(1,128)S(1)}, f32[1,256]{1,0:T(1,128)S(1)}, u32[]{:S(2)}, u32[]{:S(2)}) collective-permute-start(f32[1,256]{1,0:T(1,128)S(1)} %get-tuple-element.490), channel_id=1, source_target_pairs={{0,4},{1,5},{2,6},{3,7},{4,8},{5,9},{6,10},{7,11},{8,12},{9,13},{1... | collective-permute-start | bytes 3080 | tf_op jit(solution)/shard_map/ppermute | solution.py:20
  (136 other events, 1128.4 us)
where the time goes:
time: 842 us; the launch traced here: 833 us
  starting transfers between devices  344 us (41%)
  other arithmetic  266 us (32%)
  local copies, waits for them, and re-layouts  103 us (12%)
  loops' own time  86.1 us (10%)
  waiting for transfers between devices  29.8 us (4%)
    ppermute x180, starting transfers between devices, from_behind(): return lax.ppermute(block, axis, route)  344 us
    another operation x2, loops' own time, on_device(): lax.map(one_tile, (tile_ids, log_demand, pair_block, local_block, pair_co...  86.1 us
    dynamic_slice x96, local copies, waits for them, and re-layouts, on_device(): lax.map(one_tile, (tile_ids, log_demand, pair_block, local_block, pair_co...  60.2 us
    reduce_sum x32, other arithmetic, tile_pass(): row_sum = jnp.sum(jnp.exp(scores - row_top[None, :, None]), axis=(0, 2))  59.7 us
    reduce_sum x32, other arithmetic, tile_pass(): col_sum = jnp.sum(jnp.exp(column_scores - col_top[:, None, :]), axis=1)  52.5 us
    reduce_max x32, other arithmetic, tile_pass(): row_top = jnp.max(scores, axis=(0, 2))  46.9 us
    reduce_max x32, other arithmetic, tile_pass(): col_top = jnp.max(column_scores, axis=1)  39.1 us
    ppermute x180, waiting for transfers between devices, from_behind(): return lax.ppermute(block, axis, route)  29.8 us
  transfers between devices with their start and end apart: 180, of which 23 were waited for; matrix products, arithmetic and copies ran while one was open for 0% of the time, Pallas kernels for 0%

commit v1 on v0

v1 whole, which is shorter than its diff:
```python
import functools

import jax
import jax.numpy as jnp
from jax import lax
from jax.experimental import pallas as pl
from jax.experimental.pallas import tpu as pltpu
from jax.sharding import PartitionSpec as P

TSIDE = 16
TILE_COLS = 16
KSLOTS = 16
ITERS = 2
REACH = 64
SPAN = 16

CELLS = TSIDE * TSIDE
SCALE = 1.0 / float(REACH * REACH)
LOWEST = -1e30


def split(value):
    high = value.astype(jnp.bfloat16)
    low = (value - high.astype(jnp.float32)).astype(jnp.bfloat16)
    return high, low


def matmul(left, right_high, right_low, dims):
    rows = left.shape[0]
    high, low = split(left)
    dot = functools.partial(
        lax.dot_general, dimension_numbers=(dims, ((), ())), preferred_element_type=jnp.float32
    )
    both = dot(jnp.concatenate([high, low], axis=0), right_high)
    return both[:rows] + both[rows:] + dot(high, right_low)


def kernel(
    n,
    reach,
    window,
    demand_ref,
    cap_ref,
    warm_ref,
    xy_ref,
    pair_ref,
    count_ref,
    cell_ref,
    fac_ref,
    g_high,
    g_low,
    centre_cost,
    pots,
    part,
    land,
    mine,
    send_sem,
    recv_sem,
):
    me = lax.axis_index("tile")
    tiles = demand_ref.shape[0]
    facs = cap_ref.shape[1]
    everyone = window == n

    def first_of(device):
        return 0 if everyone else jnp.clip(device - reach, 0, n - window)

    first = first_of(me)
    here = me - first
    if everyone:
        offsets = list(range(1, n))
    else:
        offsets = [k for d in range(1, reach + 1) for k in (d, -d)]

    def each_peer(action):
        for index, offset in enumerate(offsets):
            if everyone:
                action(index, lax.rem(me + offset, n))
            else:
                peer = me + offset

                @pl.when((peer >= 0) & (peer < n))
                def _():
                    action(index, peer)

    if not everyone:
        pots[...] = jnp.zeros_like(pots)
        land[...] = jnp.full_like(land, LOWEST)

    barrier = pltpu.get_barrier_semaphore()
    each_peer(
        lambda index, peer: pl.semaphore_signal(
            barrier, inc=1, device_id={"tile": peer}, device_id_type=pl.DeviceIdType.MESH
        )
    )

    def outgoing(phase, source, target, index, peer):
        slot = me - first_of(peer)
        return pltpu.make_async_remote_copy(
            src_ref=source(peer),
            dst_ref=target.at[slot],
            send_sem=send_sem.at[phase, index],
            recv_sem=recv_sem.at[phase, slot],
            device_id={"tile": peer},
            device_id_type=pl.DeviceIdType.MESH,
        )

    def send(phase, source, target):
        each_peer(lambda index, peer: outgoing(phase, source, target, index, peer).start())

    def receive(phase, target):
        def one(index, peer):
            slot = peer - first
            pltpu.make_async_remote_copy(
                src_ref=target.at[slot],
                dst_ref=target.at[slot],
                send_sem=send_sem.at[phase, index],
                recv_sem=recv_sem.at[phase, slot],
                device_id={"tile": peer},
                device_id_type=pl.DeviceIdType.MESH,
            ).wait_recv()

        each_peer(one)

    def sent(phase, source, target):
        each_peer(lambda index, peer: outgoing(phase, source, target, index, peer).wait_send())

    tile_ids = lax.broadcasted_iota(jnp.int32, (tiles, 1), 0)
    counts = jnp.zeros((tiles, 1), jnp.int32)
    for tile in range(tiles):
        counts = jnp.where(tile_ids == tile, count_ref[tile], counts)
    slot_ids = lax.broadcasted_iota(jnp.int32, (tiles, KSLOTS), 1)
    active_blocks = jnp.where(slot_ids < counts, pair_ref[...], -1)

    centre_x = (tile_ids * TSIDE + TSIDE // 2).astype(jnp.float32)
    centre_y = (me * TSIDE + TSIDE // 2).astype(jnp.float32)
    side = lax.broadcasted_iota(jnp.int32, (TSIDE, 1), 0).astype(jnp.float32) - (TSIDE - 1) / 2

    pl.semaphore_wait(barrier, len(offsets) if everyone else jnp.minimum(me, reach) + jnp.minimum(n - 1 - me, reach))
    send(0, lambda peer: warm_ref, pots.at[0])
    pots[0, here] = warm_ref[...]

    @pl.loop(0, window)
    def _(slot):
        columns = pl.ds(pl.multiple_of(slot * facs, facs), facs)
        block = first + slot
        xy = xy_ref[block]
        fac_x, fac_y = xy[0:1], xy[1:2]
        hit = jnp.max(jnp.where(active_blocks == block, 1.0, 0.0), axis=1, keepdims=True)
        delta_x = centre_x - fac_x
        delta_y = centre_y - fac_y
        cost = (delta_x * delta_x + delta_y * delta_y) * SCALE
        centre_cost[:, columns] = jnp.where(hit > 0.0, cost, -LOWEST)
        along_x = jnp.exp((2 * SCALE) * side * fac_x)
        along_y = jnp.exp((2 * SCALE) * side * fac_y)
        for row in range(TSIDE):
            high, low = split(along_x * along_y[row : row + 1])
            rows = pl.ds(row * TSIDE, TSIDE)
            g_high[rows, columns] = high
            g_low[rows, columns] = low

    for step in range(ITERS):
        receive(2 * step, pots.at[step])
        potential = jnp.concatenate([pots[step, w] for w in range(window)], axis=1)
        scores = potential - centre_cost[...]
        top = jnp.max(scores, axis=1, keepdims=True)
        weights = jnp.exp(scores - top)
        sums = matmul(weights, g_high[...], g_low[...], ((1,), (1,)))
        rest = demand_ref[...] - (top + jnp.log(sums))
        if step == ITERS - 1:
            cell_ids = lax.broadcasted_iota(jnp.int32, (1, CELLS), 1)
            dx = (cell_ids % TSIDE).astype(jnp.float32) - (TSIDE - 1) / 2
            dy = (cell_ids // TSIDE).astype(jnp.float32) - (TSIDE - 1) / 2
            shift = (dx * (2.0 * centre_x + dx) + dy * (2.0 * centre_y + dy)) * SCALE
            cell_ref[...] = rest + shift
        rest_top = jnp.max(rest, axis=1, keepdims=True)
        column_sums = matmul(jnp.exp(rest - rest_top), g_high[...], g_low[...], ((1,), (0,)))
        column_scores = rest_top - centre_cost[...]
        column_top = jnp.max(column_scores, axis=0, keepdims=True)
        total = jnp.sum(jnp.exp(column_scores - column_top) * column_sums, axis=0, keepdims=True)
        partial = column_top + jnp.log(total)
        for w in range(window):
            part[step, w] = partial[:, w * facs : (w + 1) * facs]
        send(2 * step + 1, lambda peer: part.at[step, peer - first], land.at[step])
        land[step, here] = part[step, here]
        receive(2 * step + 1, land.at[step])
        parts = [land[step, w] for w in range(window)]
        own_top = functools.reduce(jnp.maximum, parts)
        own_sum = functools.reduce(jnp.add, [jnp.exp(p - own_top) for p in parts])
        facility = cap_ref[...] - (own_top + jnp.log(own_sum))
        if step == ITERS - 1:
            fac_ref[...] = facility
        else:
            mine[step] = facility
            send(2 * step + 2, lambda peer: mine.at[step], pots.at[step + 1])
            pots[step + 1, here] = facility

    sent(0, lambda peer: warm_ref, pots.at[0])
    for step in range(ITERS):
        sent(2 * step + 1, lambda peer: part.at[step, peer - first], land.at[step])
        if step < ITERS - 1:
            sent(2 * step + 2, lambda peer: mine.at[step], pots.at[step + 1])


def on_device(n, log_demand, log_capacity, warm_potential, facility_xy, pair_block, pair_count):
    tiles, cells = log_demand.shape
    blocks, facs = log_capacity.shape
    assert blocks == 1 and tiles == TILE_COLS and cells == CELLS
    reach = min(n - 1, SPAN)
    window = min(n, 2 * reach + 1)
    wide = window * facs
    vmem = pl.BlockSpec(memory_space=pltpu.VMEM)
    smem = pl.BlockSpec(memory_space=pltpu.SMEM)
    peers = n - 1 if window == n else 2 * reach
    return pl.pallas_call(
        functools.partial(kernel, n, reach, window),
        out_shape=(
            jax.ShapeDtypeStruct((tiles, cells), jnp.float32),
            jax.ShapeDtypeStruct((blocks, facs), jnp.float32),
        ),
        in_specs=[vmem] * 5 + [smem],
        out_specs=(vmem, vmem),
        scratch_shapes=[
            pltpu.VMEM((cells, wide), jnp.bfloat16),
            pltpu.VMEM((cells, wide), jnp.bfloat16),
            pltpu.VMEM((tiles, wide), jnp.float32),
            pltpu.VMEM((ITERS, window, 1, facs), jnp.float32),
            pltpu.VMEM((ITERS, window, 1, facs), jnp.float32),
            pltpu.VMEM((ITERS, window, 1, facs), jnp.float32),
            pltpu.VMEM((ITERS, 1, facs), jnp.float32),
            pltpu.SemaphoreType.DMA((2 * ITERS, peers)),
            pltpu.SemaphoreType.DMA((2 * ITERS, window)),
        ],
        compiler_params=pltpu.CompilerParams(
            collective_id=0, has_side_effects=True, vmem_limit_bytes=48 * 1024 * 1024
        ),
    )(log_demand, log_capacity, warm_potential, facility_xy, pair_block, pair_count)


def solution(mesh):
    placed = (
        P(("groups", "tile"), None),
        P(("groups", "tile"), None),
        P(("groups", "tile"), None),
        P("groups", None, None),
        P(("groups", "tile"), None),
        P(("groups", "tile")),
    )
    return jax.shard_map(
        functools.partial(on_device, mesh.shape["tile"]),
        mesh=mesh,
        in_specs=placed,
        out_specs=(P(("groups", "tile"), None), P(("groups", "tile"), None)),
        check_vma=False,
    )
```

time: 842 us -> 37.3 us (0.04); the launches traced: 833 us -> 37 us
  starting transfers between devices: 344 us -> 0 us
  other arithmetic: 266 us -> 0 us
  local copies, waits for them, and re-layouts: 103 us -> 5.35 us
  loops' own time: 86.1 us -> 0 us
  Pallas kernels: 0 us -> 31 us
  waiting for transfers between devices: 29.8 us -> 0 us
    ppermute x180 -> x0, starting transfers between devices: 344 us -> none  [from_behind(): return lax.ppermute(block, axis, route)]
    reduce_sum x64 -> x0, other arithmetic: 112 us -> none  [the longest x32 59.7 us: tile_pass(): row_sum = jnp.sum(jnp.exp(scores - row_top[None, :, None]), axis=(0, 2))]
    another operation x2 -> x0, loops' own time: 86.1 us -> none  [on_device(): lax.map(one_tile, (tile_ids, log_demand, pair_block, local_block, pair_co...]
    reduce_max x64 -> x0, other arithmetic: 86.1 us -> none  [the longest x32 46.9 us: tile_pass(): row_top = jnp.max(scores, axis=(0, 2))]
    dynamic_slice x96 -> x0, local copies, waits for them, and re-layouts: 60.2 us -> none  [on_device(): lax.map(one_tile, (tile_ids, log_demand, pair_block, local_block, pair_co...]
    gather x66 -> x0, local copies, waits for them, and re-layouts: 39.3 us -> none  [the longest x32 19 us: one_tile(): facility_xy[blocks]]
    pallas_call x0 -> x1, Pallas kernels: none -> 31 us  [on_device(): pl.pallas_call(functools.partial(kernel, n, reach, window), out_shape=(ja...]
    ppermute x180 -> x0, waiting for transfers between devices: 29.8 us -> none  [from_behind(): return lax.ppermute(block, axis, route)]
  transfers between devices with their start and end apart: 180 -> 0, of which waited for: 23 -> 0; matrix products, arithmetic and copies ran while one was open for 0% -> 0% of each run, Pallas kernels for 0% -> 0%
where the time goes in v1:
time: 37.3 us; the launch traced here: 37 us
  Pallas kernels  31 us (83%)
  local copies, waits for them, and re-layouts  5.35 us (14%)
  between operations  0.65 us (2%)
    pallas_call x1, Pallas kernels, on_device(): pl.pallas_call(functools.partial(kernel, n, reach, window), out_shape=(ja...  31 us
    unnamed x14, local copies, waits for them, and re-layouts  5.35 us

profile of v1, /device:TPU:0, one launch (start us, length us, event | category | flops | bytes accessed | tf_op | source)
XLA Modules:
  0.0 37.0 jit_solution(7571716103933914791)
XLA Ops:
  0.6 0.0 copy-start
  0.6 0.7 %copy-done = f32[16,2,256]{2,1,0:T(2,128)S(1)} copy-done((f32[16,2,256]{2,1,0:T(2,128)S(1)}, f32[16,2,256]{2,1,0:T(2,128)}, u32[]{:S(2)}) %copy-start) | copy-done | bytes 32792
  1.4 0.0 copy-start.1
  1.4 0.7 %copy-done.1 = f32[16,256]{1,0:T(8,128)S(1)} copy-done((f32[16,256]{1,0:T(8,128)S(1)}, f32[16,256]{1,0:T(8,128)}, u32[]{:S(2)}) %copy-start.1) | copy-done | bytes 16408
  2.1 0.0 copy-start.2
  2.1 0.7 %copy-done.2 = s32[16,16]{1,0:T(8,128)S(1)} copy-done((s32[16,16]{1,0:T(8,128)S(1)}, s32[16,16]{1,0:T(8,128)}, u32[]{:S(2)}) %copy-start.2) | copy-done | bytes 1048
  2.8 0.0 copy-start.3
  2.8 0.7 %copy-done.3 = f32[1,256]{1,0:T(1,128)S(1)} copy-done((f32[1,256]{1,0:T(1,128)S(1)}, f32[1,256]{1,0:T(1,128)}, u32[]{:S(2)}) %copy-start.3) | copy-done | bytes 1048
  3.5 0.0 copy-start.4
  3.5 0.7 %copy-done.4 = f32[1,256]{1,0:T(1,128)S(1)} copy-done((f32[1,256]{1,0:T(1,128)S(1)}, f32[1,256]{1,0:T(1,128)}, u32[]{:S(2)}) %copy-start.4) | copy-done | bytes 1048
  4.2 0.0 copy-start.5
  4.2 0.7 %copy-done.5 = s32[16]{0:T(128)S(1)} copy-done((s32[16]{0:T(128)S(1)}, s32[16]{0:T(128)}, u32[]{:S(2)}) %copy-start.5) | copy-done | bytes 88
  4.8 31.0 %shard_map.77 = (f32[16,256]{1,0:T(8,128)S(1)}, f32[1,256]{1,0:T(1,128)S(1)}) custom-call(f32[16,256]{1,0:T(8,128)S(1)} %copy-done.1, f32[1,256]{1,0:T(1,128)S(1)} %copy-done.3, f32[1,256]{1,0:T(1,128)S(1)} %copy-done.4, f32[16,2,256]{2,1,0:T(2,128)S(1)} %copy-done, s32[16,16]{1,0:T(8,128)S(1)} %copy-done.2, s32[16]{0:T(128)S(1)} %copy-done.5), custom_call_target="tpu_custom_call" | custom-call | tf_op jit(solution)/shard_map/pallas_call | solution.py:215
  35.8 0.6 %copy.10 = f32[16,256]{1,0:T(8,128)} copy(f32[16,256]{1,0:T(8,128)S(1)} %get-tuple-element.4) | data formatting | bytes 32768
  36.4 0.6 %copy.11 = f32[1,256]{1,0:T(1,128)} copy(f32[1,256]{1,0:T(1,128)S(1)} %get-tuple-element.5) | data formatting | bytes 2048
Async XLA Ops:
  0.6 0.8 %copy-start = (f32[16,2,256]{2,1,0:T(2,128)S(1)}, f32[16,2,256]{2,1,0:T(2,128)}, u32[]{:S(2)}) copy-start(f32[16,2,256]{2,1,0:T(2,128)} %xy_ref.1) | copy-start | bytes 98308
  1.4 0.7 %copy-start.1 = (f32[16,256]{1,0:T(8,128)S(1)}, f32[16,256]{1,0:T(8,128)}, u32[]{:S(2)}) copy-start(f32[16,256]{1,0:T(8,128)} %demand_ref.1) | copy-start | bytes 49156
  2.1 0.7 %copy-start.2 = (s32[16,16]{1,0:T(8,128)S(1)}, s32[16,16]{1,0:T(8,128)}, u32[]{:S(2)}) copy-start(s32[16,16]{1,0:T(8,128)} %pair_ref.1) | copy-start | bytes 3076
  2.8 0.7 %copy-start.3 = (f32[1,256]{1,0:T(1,128)S(1)}, f32[1,256]{1,0:T(1,128)}, u32[]{:S(2)}) copy-start(f32[1,256]{1,0:T(1,128)} %cap_ref.1) | copy-start | bytes 3076
  3.5 0.7 %copy-start.4 = (f32[1,256]{1,0:T(1,128)S(1)}, f32[1,256]{1,0:T(1,128)}, u32[]{:S(2)}) copy-start(f32[1,256]{1,0:T(1,128)} %warm_ref.1) | copy-start | bytes 3076
  4.2 0.7 %copy-start.5 = (s32[16]{0:T(128)S(1)}, s32[16]{0:T(128)}, u32[]{:S(2)}) copy-start(s32[16]{0:T(128)} %count_ref.1) | copy-start | bytes 196
